TPU v7x, 32 devices: a whole 2x2x4 slice. The times are simulated.
32 devices in a mesh: wide: 8 (over y, x, core), narrow: 4 (over z).
Axes of the slice: x: 2, y: 2, z: 4, core: 2. Of those that a mesh axis runs over, the one named last changes fastest.
Arguments:
- x_zero: bfloat16 [4608, 3456], P(('wide', 'narrow')), may hold values from -6 to 6
- labels: int32 [4608], P(('wide', 'narrow')), may hold values 0 or 1
- cross_u: bfloat16 [3456, 256], replicated, may hold values from -0.375 to 0.375
- cross_v: bfloat16 [3456, 256], replicated, may hold values from -0.109375 to 0.109375
- cross_bias: float32 [3456], replicated, may hold values from -3 to 3
- head: float32 [3456], replicated, may hold values from -0.109375 to 0.109375
- hot_table: float32 [8192, 128], replicated, may hold values from -6 to 6
- hot_acc: float32 [8192], replicated, may hold values from 0.01 to 100
- cold_table: float32 [65536, 128], P(('wide', 'narrow')), may hold values from -6 to 6
- cold_acc: float32 [65536], P(('wide', 'narrow')), may hold values from 0.0001 to 0.01
- hot_ids: int32 [4608, 26, 19], P(('wide', 'narrow')), may hold values from 0 to 8191
- cold_owner: int32 [4608, 26, 1], P(('wide', 'narrow')), may hold values from 0 to 31; in each aligned block of 3744 rows (0 to 3743, 3744 to 7487, ..., all dimensions but the last counted through in order) at most 468 rows name the same one
- cold_slot: int32 [4608, 26], P(('wide', 'narrow')), may hold values from 0 to 2047
Outputs:
- hot_out: float32 [8192, 128], replicated
- cold_out: float32 [65536, 128], P(('wide', 'narrow'))
- grad_u: bfloat16 [3456, 256], replicated
- grad_v: bfloat16 [3456, 256], replicated
- grad_bias: float32 [3456], replicated
Inputs may be any that keep to these rules, and one draw needn't show every extreme that they name: `cold_owner`: an owner is a device's index over wide and narrow, wide slowest. Among the 3744 bags of one device no owner is named by more than 468 bags, a bound that some block reaches.
All inputs are finite; a program needn't handle non-finite values. No bound on the sum of `labels` on one device may be relied on, other than what follows from the above.
Results may differ from a plain program's by a relative error of at most 0.0058.
Values may be sent and summed in bfloat16 or wider, within the bound.
A program may use at most 128 MiB of HBM per device.

v0:
```python
import math
import jax
import jax.numpy as jnp
from jax import lax
from jax.sharding import PartitionSpec as P

LEARN_RATE = 0.5
EPSILON = 1e-08


def adagrad_rows(table, accum, grad):
    new_acc = accum + jnp.mean(grad * grad, axis=1)
    return table - LEARN_RATE * grad / (jnp.sqrt(new_acc)[:, None] + EPSILON)


def per_device(
    x_zero,
    labels,
    cross_u,
    cross_v,
    cross_bias,
    head,
    hot_table,
    hot_acc,
    cold_table,
    cold_acc,
    hot_ids,
    cold_owner,
    cold_slot,
):
    samples = x_zero.shape[0]
    emb_width = cold_table.shape[1]
    features = hot_ids.shape[1]
    lanes = hot_ids.shape[2]
    shard_rows = cold_table.shape[0]
    hot_rows_all = hot_table.shape[0]
    bag_count = samples * features
    proj_b = jnp.dot(x_zero, cross_v, preferred_element_type=jnp.float32).astype(jnp.bfloat16)
    mixed = jnp.dot(proj_b, cross_u.T, preferred_element_type=jnp.float32)
    scale = mixed + cross_bias[None, :]
    x_float = x_zero.astype(jnp.float32)
    crossed = x_float * scale + x_float
    logit = jnp.sum(crossed * head[None, :], axis=1)
    delta = jax.nn.sigmoid(logit) - labels.astype(jnp.float32)
    upstream = delta[:, None] * head[None, :]
    dscale = upstream * x_float
    dscale_b = dscale.astype(jnp.bfloat16)
    dproj_b = jnp.dot(dscale_b, cross_u, preferred_element_type=jnp.float32).astype(jnp.bfloat16)
    pooled = upstream[:, emb_width:] * (scale[:, emb_width:] + 1.0) + jnp.dot(
        dproj_b, cross_v[emb_width:].T, preferred_element_type=jnp.float32
    )
    flat_b = pooled.astype(jnp.bfloat16).reshape(bag_count, emb_width)
    owners = cold_owner.reshape(bag_count)
    places = cold_slot.reshape(bag_count)
    devices = lax.axis_size(("wide", "narrow"))
    capacity = 4 * bag_count // devices
    order = jnp.argsort(owners, stable=True)
    sorted_owner = owners[order]
    counts = jnp.sum(
        (owners[:, None] == jnp.arange(devices, dtype=jnp.int32)[None, :]).astype(jnp.int32), axis=0
    )
    starts = jnp.cumsum(counts) - counts
    position = jnp.arange(bag_count, dtype=jnp.int32) - starts[sorted_owner]
    target = sorted_owner * capacity + position
    send_grad = (
        jnp.zeros((devices * capacity, emb_width), jnp.bfloat16).at[target].set(flat_b[order])
    )
    send_place = jnp.zeros((devices * capacity,), jnp.int32).at[target].set(places[order])
    recv_grad, recv_place = (
        lax.all_to_all(
            send_grad.reshape(devices, capacity, emb_width),
            ("wide", "narrow"),
            split_axis=0,
            concat_axis=0,
            tiled=True,
        ),
        lax.all_to_all(
            send_place.reshape(devices, capacity),
            ("wide", "narrow"),
            split_axis=0,
            concat_axis=0,
            tiled=True,
        ),
    )
    recv_rows = recv_grad.reshape(-1, emb_width)
    recv_where = recv_place.reshape(-1)
    slot_block = math.gcd(shard_rows, 512)

    def cold_block(first):
        columns = first + jnp.arange(slot_block, dtype=jnp.int32)
        onehot = (recv_where[:, None] == columns[None, :]).astype(jnp.bfloat16)
        return lax.dot_general(
            onehot, recv_rows, (((0,), (0,)), ((), ())), preferred_element_type=jnp.float32
        )

    cold_firsts = jnp.arange(0, shard_rows, slot_block, dtype=jnp.int32)
    cold_grad = lax.map(cold_block, cold_firsts).reshape(shard_rows, emb_width)
    cold_out = adagrad_rows(cold_table, cold_acc, cold_grad)
    flat_ids = hot_ids.reshape(bag_count, lanes)
    hot_block = math.gcd(hot_rows_all, 1024)

    def hot_part(first):
        columns = first + jnp.arange(hot_block, dtype=jnp.int32)
        tally = jnp.zeros((bag_count, hot_block), jnp.bfloat16)
        for lane in range(lanes):
            tally = tally + (flat_ids[:, lane][:, None] == columns[None, :]).astype(jnp.bfloat16)
        return lax.dot_general(
            tally, flat_b, (((0,), (0,)), ((), ())), preferred_element_type=jnp.float32
        )

    hot_firsts = jnp.arange(0, hot_rows_all, hot_block, dtype=jnp.int32)
    hot_local = lax.map(hot_part, hot_firsts).reshape(hot_rows_all, emb_width)
    part_u = lax.dot_general(
        dscale_b, proj_b, (((0,), (0,)), ((), ())), preferred_element_type=jnp.float32
    )
    part_v = lax.dot_general(
        x_zero, dproj_b, (((0,), (0,)), ((), ())), preferred_element_type=jnp.float32
    )
    part_c = jnp.sum(dscale, axis=0)
    hot_grad, sum_u, sum_v, sum_c = lax.psum(
        (hot_local, part_u, part_v, part_c), ("wide", "narrow")
    )
    hot_out = adagrad_rows(hot_table, hot_acc, hot_grad)
    return (hot_out, cold_out, sum_u.astype(jnp.bfloat16), sum_v.astype(jnp.bfloat16), sum_c)


def solution(mesh):
    placed = (
        P(("wide", "narrow"), None),
        P(("wide", "narrow")),
        P(),
        P(),
        P(),
        P(),
        P(),
        P(),
        P(("wide", "narrow"), None),
        P(("wide", "narrow")),
        P(("wide", "narrow"), None, None),
        P(("wide", "narrow"), None, None),
        P(("wide", "narrow"), None),
    )
    return jax.shard_map(
        per_device,
        mesh=mesh,
        in_specs=placed,
        out_specs=(P(), P(("wide", "narrow"), None), P(), P(), P()),
        check_vma=False,
    )
```

profile of v0, /device:TPU:0, one launch (start us, length us, event | category | flops | bytes accessed | tf_op | source)
XLA Modules:
  0.0 670.6 jit_solution(11999604817901376762)
XLA Ops:
  7.2 1.0 copy.32
  8.7 0.7 fusion.74
  9.4 0.7 fusion.73
  10.2 5.8 sort.17
  16.0 19.9 %gather_fusion = s32[3744]{0:T(1024)S(1)} fusion(s32[3744]{0:T(1024)S(1)} %reshape.130, s32[4096]{0:T(1024)S(1)} %pad_clamp_fusion), kind=kCustom, calls=%fused_computation | custom fusion | bytes 44928 | tf_op jit(solution)/shard_map/gather | solution.py:58
  36.2 19.9 %gather_fusion.1 = s32[3744]{0:T(1024)S(1)} fusion(s32[3744]{0:T(1024)S(1)} %reshape.133, s32[4096]{0:T(1024)S(1)} %pad_clamp_fusion), kind=kCustom, calls=%fused_computation.1 | custom fusion | bytes 44928 | tf_op jit(solution)/shard_map/gather | solution.py:68
  56.1 4.4 fusion.71
  60.5 1.1 compare_reduce_fusion.24
  61.6 15.8 %select_select_fusion = s32[3744]{0:T(1024)S(1)} fusion(pred[3744]{0:T(1024)(128)(4,1)S(1)} %get-tuple-element.126, pred[3744]{0:T(1024)(128)(4,1)S(1)} %get-tuple-element.125, pred[3744]{0:T(1024)(128)(4,1)S(1)} %get-tuple-element.124, pred[3744]{0:T(1024)(128)(4,1)S(1)} %get-tuple-element.123, pred[3744]{0:T(1024)(128)(4,1)S(1)} %get-tuple-element.122, ...), kind=kLoop, calls=%fused_computation.158 | loop fusion | flops 93600 | bytes 123652 | tf_op jit(solution)/shard_map/gather | solution.py:63
  77.5 18.2 %scatter_custom_fusion = s32[14976]{0:T(1024)S(1)} fusion(s32[3744]{0:T(1024)S(1)} %fusion.72, s32[3744]{0:T(1024)S(1)} %gather_fusion.1, s32[]{:T(128)} %copy.60), kind=kCustom, calls=%fused_computation.155 | custom fusion | bytes 59908 | tf_op jit(solution)/shard_map/scatter | solution.py:68
  95.7 0.8 all_to_all.11
  96.5 7.9 %all-to-all-start = ((s32[32,1,468]{2,1,0:T(1,128)}), s32[32,1,468]{2,1,0:T(1,128)}, u32[]{:S(2)}, u32[]{:S(2)}) async-start(s32[32,1,468]{2,1,0:T(1,128)} %all_to_all.11), calls=%async_computation | async-start | bytes 131072 | tf_op jit(solution)/shard_map/all_to_all | solution.py:77
  104.4 1.9 convolution_convert_fusion.1
  106.4 0.9 fusion.57
  107.9 1.0 fusion.62
  108.8 1.7 fusion.55
  110.6 1.6 copy.31
  112.1 0.6 reshape.127
  112.8 2.3 reshape.128
  115.1 30.2 %scatter_custom_fusion.1 = bf16[14976,128]{1,0:T(8,128)(2,1)} fusion(s32[3744]{0:T(1024)} %copy-done.17, bf16[]{:T(256)} %constant.18.clone.1, bf16[3744,128]{1,0:T(8,128)(2,1)S(1)} %reshape.128, s32[4096]{0:T(1024)S(1)} %pad_clamp_fusion), kind=kCustom, calls=%fused_computation.103 | custom fusion | bytes 3834368 | tf_op jit(solution)/shard_map/scatter | solution.py:66
  145.3 5.8 reshape.134
  151.1 6.1 all-to-all-start.1
  157.4 267.2 %while.21 = (s32[]{:T(128)}, f32[8,1024,128]{2,1,0:T(8,128)}, s32[3744,19]{0,1:T(8,128)S(1)}, s32[8]{0:T(128)S(1)}, bf16[3744,128]{1,0:T(8,128)(2,1)S(1)}, /*index=5*/s32[]{:T(128)}) while((s32[]{:T(128)}, f32[8,1024,128]{2,1,0:T(8,128)}, s32[3744,19]{0,1:T(8,128)S(1)}, s32[8]{0:T(128)S(1)}, bf16[3744,128]{1,0:T(8,128)(2,1)S(1)}, ...), condition=%wide.region_2.3_spmd, body=%wide.region_1.0_spmd.sunk | while | flops 1196164096 | bytes 2344673 | solution.py:112
  157.4 0.6 dynamic_slice.11
  158.0 0.6 iota_add_fusion.5
  158.6 0.8 slice_reduce_fusion.20
  159.4 31.4 %fusion.100 = f32[8,1024,128]{2,1,0:T(8,128)} fusion(f32[8,1024,128]{2,1,0:T(8,128)} %get-tuple-element.323, s32[]{:T(128)S(6)} %copy.44, bf16[3744,128]{1,0:T(8,128)(2,1)S(1)} %get-tuple-element.332, s32[1024]{0:T(1024)S(1)} %iota_add_fusion.5, s32[3744]{0:T(1024)S(1)} %get-tuple-element.291, s32[3744]{0:T(1024)S(1)} %get-tuple-element.292, ...), kind=kOutput, calls=%fused_computation.70.clone.2 | convolution fusion | flops 1196163072 | bytes 1771396 | tf_op jit(solution)/shard_map/while/body/eval_jaxpr/dot_general | solution.py:107
  191.4 0.6 iota_add_fusion.5
  192.0 0.8 slice_reduce_fusion.20
  192.8 31.4 %fusion.100 = f32[8,1024,128]{2,1,0:T(8,128)} fusion(f32[8,1024,128]{2,1,0:T(8,128)} %get-tuple-element.323, s32[]{:T(128)S(6)} %copy.44, bf16[3744,128]{1,0:T(8,128)(2,1)S(1)} %get-tuple-element.332, s32[1024]{0:T(1024)S(1)} %iota_add_fusion.5, s32[3744]{0:T(1024)S(1)} %get-tuple-element.291, s32[3744]{0:T(1024)S(1)} %get-tuple-element.292, ...), kind=kOutput, calls=%fused_computation.70.clone.2 | convolution fusion | flops 1196163072 | bytes 1771396 | tf_op jit(solution)/shard_map/while/body/eval_jaxpr/dot_general | solution.py:107
  224.8 0.6 iota_add_fusion.5
  225.4 0.8 slice_reduce_fusion.20
  226.2 31.4 %fusion.100 = f32[8,1024,128]{2,1,0:T(8,128)} fusion(f32[8,1024,128]{2,1,0:T(8,128)} %get-tuple-element.323, s32[]{:T(128)S(6)} %copy.44, bf16[3744,128]{1,0:T(8,128)(2,1)S(1)} %get-tuple-element.332, s32[1024]{0:T(1024)S(1)} %iota_add_fusion.5, s32[3744]{0:T(1024)S(1)} %get-tuple-element.291, s32[3744]{0:T(1024)S(1)} %get-tuple-element.292, ...), kind=kOutput, calls=%fused_computation.70.clone.2 | convolution fusion | flops 1196163072 | bytes 1771396 | tf_op jit(solution)/shard_map/while/body/eval_jaxpr/dot_general | solution.py:107
  258.2 0.6 iota_add_fusion.5
  258.8 0.8 slice_reduce_fusion.20
  259.6 31.4 %fusion.100 = f32[8,1024,128]{2,1,0:T(8,128)} fusion(f32[8,1024,128]{2,1,0:T(8,128)} %get-tuple-element.323, s32[]{:T(128)S(6)} %copy.44, bf16[3744,128]{1,0:T(8,128)(2,1)S(1)} %get-tuple-element.332, s32[1024]{0:T(1024)S(1)} %iota_add_fusion.5, s32[3744]{0:T(1024)S(1)} %get-tuple-element.291, s32[3744]{0:T(1024)S(1)} %get-tuple-element.292, ...), kind=kOutput, calls=%fused_computation.70.clone.2 | convolution fusion | flops 1196163072 | bytes 1771396 | tf_op jit(solution)/shard_map/while/body/eval_jaxpr/dot_general | solution.py:107
  291.6 0.6 iota_add_fusion.5
  292.2 0.8 slice_reduce_fusion.20
  293.0 31.4 %fusion.100 = f32[8,1024,128]{2,1,0:T(8,128)} fusion(f32[8,1024,128]{2,1,0:T(8,128)} %get-tuple-element.323, s32[]{:T(128)S(6)} %copy.44, bf16[3744,128]{1,0:T(8,128)(2,1)S(1)} %get-tuple-element.332, s32[1024]{0:T(1024)S(1)} %iota_add_fusion.5, s32[3744]{0:T(1024)S(1)} %get-tuple-element.291, s32[3744]{0:T(1024)S(1)} %get-tuple-element.292, ...), kind=kOutput, calls=%fused_computation.70.clone.2 | convolution fusion | flops 1196163072 | bytes 1771396 | tf_op jit(solution)/shard_map/while/body/eval_jaxpr/dot_general | solution.py:107
  325.0 0.6 iota_add_fusion.5
  325.6 0.8 slice_reduce_fusion.20
  326.4 31.4 %fusion.100 = f32[8,1024,128]{2,1,0:T(8,128)} fusion(f32[8,1024,128]{2,1,0:T(8,128)} %get-tuple-element.323, s32[]{:T(128)S(6)} %copy.44, bf16[3744,128]{1,0:T(8,128)(2,1)S(1)} %get-tuple-element.332, s32[1024]{0:T(1024)S(1)} %iota_add_fusion.5, s32[3744]{0:T(1024)S(1)} %get-tuple-element.291, s32[3744]{0:T(1024)S(1)} %get-tuple-element.292, ...), kind=kOutput, calls=%fused_computation.70.clone.2 | convolution fusion | flops 1196163072 | bytes 1771396 | tf_op jit(solution)/shard_map/while/body/eval_jaxpr/dot_general | solution.py:107
  358.4 0.6 iota_add_fusion.5
  359.1 0.8 slice_reduce_fusion.20
  359.8 31.4 %fusion.100 = f32[8,1024,128]{2,1,0:T(8,128)} fusion(f32[8,1024,128]{2,1,0:T(8,128)} %get-tuple-element.323, s32[]{:T(128)S(6)} %copy.44, bf16[3744,128]{1,0:T(8,128)(2,1)S(1)} %get-tuple-element.332, s32[1024]{0:T(1024)S(1)} %iota_add_fusion.5, s32[3744]{0:T(1024)S(1)} %get-tuple-element.291, s32[3744]{0:T(1024)S(1)} %get-tuple-element.292, ...), kind=kOutput, calls=%fused_computation.70.clone.2 | convolution fusion | flops 1196163072 | bytes 1771396 | tf_op jit(solution)/shard_map/while/body/eval_jaxpr/dot_general | solution.py:107
  391.8 0.6 iota_add_fusion.5
  392.5 0.8 slice_reduce_fusion.20
  393.2 31.4 %fusion.100 = f32[8,1024,128]{2,1,0:T(8,128)} fusion(f32[8,1024,128]{2,1,0:T(8,128)} %get-tuple-element.323, s32[]{:T(128)S(6)} %copy.44, bf16[3744,128]{1,0:T(8,128)(2,1)S(1)} %get-tuple-element.332, s32[1024]{0:T(1024)S(1)} %iota_add_fusion.5, s32[3744]{0:T(1024)S(1)} %get-tuple-element.291, s32[3744]{0:T(1024)S(1)} %get-tuple-element.292, ...), kind=kOutput, calls=%fused_computation.70.clone.2 | convolution fusion | flops 1196163072 | bytes 1771396 | tf_op jit(solution)/shard_map/while/body/eval_jaxpr/dot_general | solution.py:107
  424.7 1.1 copy-done.2
  425.8 2.6 fusion.66
  428.4 2.5 convolution_bitcast_fusion
  430.9 156.5 %all-reduce.5 = (bf16[3456,256]{1,0:T(8,128)(2,1)}, bf16[3456,256]{0,1:T(8,128)(2,1)S(1)}, f32[3456]{0:T(1024)}) all-reduce(f32[3456,256]{1,0:T(8,128)} %fusion.66, f32[3456,256]{0,1:T(8,128)} %convolution_bitcast_fusion, f32[3456]{0:T(1024)S(1)} %copy-done.13), channel_id=1, replica_groups=mesh['wide'=8,'narrow'=4] {'wide','narrow'}, use_global_device_ids=true, to_apply=%region_13.14 | all-reduce | flops 1772928 | bytes 10644480 | tf_op jit(solution)/shard_map/psum | solution.py:120
  587.4 2.2 copy.35
  589.6 0.9 copy.39
  590.7 3.5 multiply_reduce_fusion
  594.2 4.2 divide_subtract_fusion
  598.4 5.8 reshape.135
  604.3 56.4 %while.22 = (s32[]{:T(128)}, f32[4,512,128]{2,1,0:T(8,128)}, s32[32,468]{1,0:T(8,128)}, s32[4]{0:T(128)S(1)}, bf16[14976,128]{1,0:T(8,128)(2,1)}, /*index=5*/s32[14976]{0:T(1024)S(1)}, s32[]{:T(128)}) while((s32[]{:T(128)}, f32[4,512,128]{2,1,0:T(8,128)}, s32[32,468]{1,0:T(8,128)}, s32[4]{0:T(128)S(1)}, ...), condition=%wide.wide.region_11.12_spmd, body=%wide.wide.region_10.11_spmd.sunk | while | flops 1970602496 | bytes 4160105 | solution.py:97
  605.6 12.9 %fusion.103 = f32[4,512,128]{2,1,0:T(8,128)} fusion(f32[4,512,128]{2,1,0:T(8,128)} %get-tuple-element.342, s32[]{:T(128)S(6)} %copy.51, bf16[14976,128]{1,0:T(8,128)(2,1)} %get-tuple-element.352, s32[512]{0:T(512)S(1)} %iota_add_fusion.6, s32[14976]{0:T(1024)S(1)} %get-tuple-element.353), kind=kOutput, calls=%fused_computation.10.clone.clone.1 | convolution fusion | flops 1970601984 | bytes 4157956 | tf_op jit(solution)/shard_map/while/body/eval_jaxpr/dot_general | solution.py:92
  619.6 12.9 %fusion.103 = f32[4,512,128]{2,1,0:T(8,128)} fusion(f32[4,512,128]{2,1,0:T(8,128)} %get-tuple-element.342, s32[]{:T(128)S(6)} %copy.51, bf16[14976,128]{1,0:T(8,128)(2,1)} %get-tuple-element.352, s32[512]{0:T(512)S(1)} %iota_add_fusion.6, s32[14976]{0:T(1024)S(1)} %get-tuple-element.353), kind=kOutput, calls=%fused_computation.10.clone.clone.1 | convolution fusion | flops 1970601984 | bytes 4157956 | tf_op jit(solution)/shard_map/while/body/eval_jaxpr/dot_general | solution.py:92
  633.7 12.9 %fusion.103 = f32[4,512,128]{2,1,0:T(8,128)} fusion(f32[4,512,128]{2,1,0:T(8,128)} %get-tuple-element.342, s32[]{:T(128)S(6)} %copy.51, bf16[14976,128]{1,0:T(8,128)(2,1)} %get-tuple-element.352, s32[512]{0:T(512)S(1)} %iota_add_fusion.6, s32[14976]{0:T(1024)S(1)} %get-tuple-element.353), kind=kOutput, calls=%fused_computation.10.clone.clone.1 | convolution fusion | flops 1970601984 | bytes 4157956 | tf_op jit(solution)/shard_map/while/body/eval_jaxpr/dot_general | solution.py:92
  647.7 12.9 %fusion.103 = f32[4,512,128]{2,1,0:T(8,128)} fusion(f32[4,512,128]{2,1,0:T(8,128)} %get-tuple-element.342, s32[]{:T(128)S(6)} %copy.51, bf16[14976,128]{1,0:T(8,128)(2,1)} %get-tuple-element.352, s32[512]{0:T(512)S(1)} %iota_add_fusion.6, s32[14976]{0:T(1024)S(1)} %get-tuple-element.353), kind=kOutput, calls=%fused_computation.10.clone.clone.1 | convolution fusion | flops 1970601984 | bytes 4157956 | tf_op jit(solution)/shard_map/while/body/eval_jaxpr/dot_general | solution.py:92
  660.6 1.6 multiply_reduce_fusion.1
  662.2 1.3 fusion.64
  (86 shorter events, 10.5 us)
Async XLA Ops:
  7.2 99.2 %copy-start = (bf16[3456,256]{1,0:T(8,128)(2,1)S(1)}, bf16[3456,256]{1,0:T(8,128)(2,1)}, u32[]{:S(2)}) copy-start(bf16[3456,256]{1,0:T(8,128)(2,1)} %param.19) | copy-start | bytes 5308420
  16.0 19.9 %copy-start.15 = (s32[144,26]{0,1:T(8,128)S(1)}, s32[144,26]{0,1:T(8,128)}, u32[]{:S(2)}) copy-start(s32[144,26]{0,1:T(8,128)} %param.29) | copy-start | bytes 44932
  36.2 68.2 %copy-start.1 = (bf16[144,3456]{1,0:T(8,128)(2,1)S(1)}, bf16[144,3456]{1,0:T(8,128)(2,1)}, u32[]{:S(2)}) copy-start(bf16[144,3456]{1,0:T(8,128)(2,1)} %param.17) | copy-start | bytes 2985988
  36.2 70.2 %copy-start.11 = (f32[3456]{0:T(1024)S(1)}, f32[3456]{0:T(1024)}, u32[]{:S(2)}) copy-start(f32[3456]{0:T(1024)} %param.22) | copy-start | bytes 41476
  36.2 70.2 %copy-start.16 = (f32[3456]{0:T(1024)S(1)}, f32[3456]{0:T(1024)}, u32[]{:S(2)}) copy-start(f32[3456]{0:T(1024)} %param.21) | copy-start | bytes 41476
  77.5 29.8 %copy-start.17 = (s32[3744]{0:T(1024)}, s32[3744]{0:T(1024)S(1)}, u32[]{:S(2)}) copy-start(s32[3744]{0:T(1024)S(1)} %fusion.72) | copy-start | bytes 44932
  96.5 54.6 %all-to-all-start = ((s32[32,1,468]{2,1,0:T(1,128)}), s32[32,1,468]{2,1,0:T(1,128)}, u32[]{:S(2)}, u32[]{:S(2)}) async-start(s32[32,1,468]{2,1,0:T(1,128)} %all_to_all.11), calls=%async_computation | async-start | bytes 131072 | tf_op jit(solution)/shard_map/all_to_all | solution.py:77
  104.4 2.9 copy-start.21
  106.4 1.5 copy-start.6
  107.3 1.6 copy-start.4
  107.3 3.2 copy-start.18
  107.9 1.0 copy-start.8
  151.1 447.3 %all-to-all-start.1 = ((bf16[32,468,128]{2,1,0:T(8,128)(2,1)}), bf16[32,468,128]{2,1,0:T(8,128)(2,1)}, u32[]{:S(2)}, u32[]{:S(2)}) async-start(bf16[32,468,128]{2,1,0:T(8,128)(2,1)} %reshape.134), calls=%async_computation.1 | async-start | bytes 7733248 | tf_op jit(solution)/shard_map/all_to_all | solution.py:70
  157.2 433.5 %all-reduce.4.cloned.1.call-start = ((), (), s32[]{:S(2)}) async-start(), calls=%async_computation.2 | async-start | bytes 8388608 | tf_op jit(solution)/shard_map/psum | solution.py:120
  424.6 1.2 copy-start.2
  424.6 1.2 copy-start.7
  424.6 1.2 copy-start.12
  424.6 1.2 copy-start.19
  424.6 3.8 copy-start.9
  425.8 5.1 copy-start.13
  589.6 4.5 copy-start.14
  590.5 7.9 %copy-start.10 = (s32[32,1,468]{2,0,1:T(8,128)}, s32[32,1,468]{2,0,1:T(8,128)S(1)}, u32[]{:S(2)}) copy-start(s32[32,1,468]{2,0,1:T(8,128)S(1)} %copy.39) | copy-start | bytes 179716
  590.6 3.5 copy-start.3
  604.2 58.0 %copy-start.20 = (f32[2048]{0:T(1024)S(1)}, f32[2048]{0:T(1024)}, u32[]{:S(2)}) copy-start(f32[2048]{0:T(1024)} %param.26) | copy-start | bytes 24580
  604.2 58.0 %copy-start.5 = (f32[2048,128]{1,0:T(8,128)S(1)}, f32[2048,128]{1,0:T(8,128)}, u32[]{:S(2)}) copy-start(f32[2048,128]{1,0:T(8,128)} %param.25) | copy-start | bytes 3145732
Sparse Core Ops, SparseCore 0:
  424.8 151.6 all-reduce.3
where the time goes:
time: 677 us; the launch traced here: 671 us
  matrix products  313 us (46%)
  blocking collectives  156 us (23%)
  local copies, waits for them, and re-layouts  125 us (18%)
  other arithmetic  46.6 us (7%)
  between operations  14.7 us (2%)
  starting transfers between devices  14.2 us (2%)
    dot_general x8, matrix products, hot_part(): lax.dot_general(tally, flat_b, (((0,), (0,)), ((), ())), preferred_elemen...  251 us
    psum x1, blocking collectives, per_device(): lax.psum((hot_local, part_u, part_v, part_c), ('wide', 'narrow'))  156 us
    dot_general x4, matrix products, cold_block(): lax.dot_general(onehot, recv_rows, (((0,), (0,)), ((), ())), preferred_el...  51.6 us
    scatter x1, local copies, waits for them, and re-layouts, per_device(): jnp.zeros((devices * capacity, emb_width), jnp.bfloat16).at[target]  30.2 us
    gather x3, other arithmetic, per_device(): position = jnp.arange(bag_count, dtype=jnp.int32) - starts[sorted_owner]  21.3 us
    gather x1, local copies, waits for them, and re-layouts, per_device(): sorted_owner = owners[order]  19.9 us
    gather x1, local copies, waits for them, and re-layouts, per_device(): places[order]  19.9 us
    scatter x1, local copies, waits for them, and re-layouts, per_device(): jnp.zeros((devices * capacity,), jnp.int32).at[target].set(places[order])  18.2 us
  transfers between devices with their start and end apart: 3, of which 0 were waited for; matrix products, arithmetic and copies ran while one was open for 49% of the time, Pallas kernels for 0%

commit v1 on v0

--- a/solution.py
+++ b/solution.py
@@ -118,7 +118,7 @@
     )
     part_c = jnp.sum(dscale, axis=0)
     hot_grad, sum_u, sum_v, sum_c = lax.psum(
-        (hot_local, part_u, part_v, part_c), ("wide", "narrow")
+        lax.psum((hot_local, part_u, part_v, part_c), "narrow"), "wide"
     )
     hot_out = adagrad_rows(hot_table, hot_acc, hot_grad)
     return (hot_out, cold_out, sum_u.astype(jnp.bfloat16), sum_v.astype(jnp.bfloat16), sum_c)

time: 677 us -> 1030 us (1.52)
  waiting for transfers between devices: 0.04 us -> 302 us
  blocking collectives: 156 us -> 208 us
    psum x1 -> x2, waiting for transfers between devices: 0.02 us -> 302 us  [the longest x1 302 us: per_device(): lax.psum((hot_local, part_u, part_v, part_c), 'narrow')]
    psum x1 -> x2, blocking collectives: 156 us -> 208 us  [the longest x1 188 us: per_device(): lax.psum(lax.psum((hot_local, part_u, part_v, part_c), 'narrow'), 'wide')]
  transfers between devices with their start and end apart: 3 -> 4, of which waited for: 0 -> 1; matrix products, arithmetic and copies ran while one was open for 49% -> 38% of each run, Pallas kernels for 0% -> 0%
where the time goes in v1:
time: 1030 us; the launch traced here: 1020 us
  matrix products  312 us (30%)
  waiting for transfers between devices  302 us (29%)
  blocking collectives  208 us (20%)
  local copies, waits for them, and re-layouts  123 us (12%)
  other arithmetic  47.2 us (5%)
  between operations  14.8 us (1%)
  starting transfers between devices  14.1 us (1%)
    psum x1, waiting for transfers between devices, per_device(): lax.psum((hot_local, part_u, part_v, part_c), 'narrow')  302 us
    dot_general x8, matrix products, hot_part(): lax.dot_general(tally, flat_b, (((0,), (0,)), ((), ())), preferred_elemen...  251 us
    psum x1, blocking collectives, per_device(): lax.psum(lax.psum((hot_local, part_u, part_v, part_c), 'narrow'), 'wide')  188 us
    dot_general x4, matrix products, cold_block(): lax.dot_general(onehot, recv_rows, (((0,), (0,)), ((), ())), preferred_el...  51.7 us
    scatter x1, local copies, waits for them, and re-layouts, per_device(): jnp.zeros((devices * capacity, emb_width), jnp.bfloat16).at[target]  30.1 us
    gather x3, other arithmetic, per_device(): position = jnp.arange(bag_count, dtype=jnp.int32) - starts[sorted_owner]  21.3 us
  transfers between devices with their start and end apart: 4, of which 1 were waited for; matrix products, arithmetic and copies ran while one was open for 38% of the time, Pallas kernels for 0%

profile of v1, /device:TPU:0, one launch (start us, length us, event | category | flops | bytes accessed | tf_op | source)
XLA Modules:
  0.0 1021.2 jit_solution(16147189925082279091)
XLA Ops:
  7.2 1.0 copy.32
  8.7 0.7 fusion.74
  9.4 0.7 fusion.73
  10.2 5.8 sort.17
  16.0 19.9 %gather_fusion = s32[3744]{0:T(1024)S(1)} fusion(s32[3744]{0:T(1024)S(1)} %reshape.130, s32[4096]{0:T(1024)S(1)} %pad_clamp_fusion), kind=kCustom, calls=%fused_computation | custom fusion | bytes 44928 | tf_op jit(solution)/shard_map/gather | solution.py:58
  35.9 4.4 fusion.71
  40.3 1.1 compare_reduce_fusion.24
  41.5 15.8 %select_select_fusion = s32[3744]{0:T(1024)S(1)} fusion(pred[3744]{0:T(1024)(128)(4,1)S(1)} %get-tuple-element.126, pred[3744]{0:T(1024)(128)(4,1)S(1)} %get-tuple-element.125, pred[3744]{0:T(1024)(128)(4,1)S(1)} %get-tuple-element.124, pred[3744]{0:T(1024)(128)(4,1)S(1)} %get-tuple-element.123, pred[3744]{0:T(1024)(128)(4,1)S(1)} %get-tuple-element.122, ...), kind=kLoop, calls=%fused_computation.158 | loop fusion | flops 93600 | bytes 123652 | tf_op jit(solution)/shard_map/gather | solution.py:63
  57.6 19.9 %gather_fusion.1 = s32[3744]{0:T(1024)S(1)} fusion(s32[3744]{0:T(1024)S(1)} %reshape.133, s32[4096]{0:T(1024)S(1)} %pad_clamp_fusion), kind=kCustom, calls=%fused_computation.1 | custom fusion | bytes 44928 | tf_op jit(solution)/shard_map/gather | solution.py:68
  77.5 18.2 %scatter_custom_fusion = s32[14976]{0:T(1024)S(1)} fusion(s32[3744]{0:T(1024)S(1)} %fusion.72, s32[3744]{0:T(1024)S(1)} %gather_fusion.1, s32[]{:T(128)} %copy.63), kind=kCustom, calls=%fused_computation.155 | custom fusion | bytes 59908 | tf_op jit(solution)/shard_map/scatter | solution.py:68
  95.7 0.8 all_to_all.11
  96.5 7.8 all-to-all-start
  104.3 1.9 convolution_convert_fusion.1
  106.3 0.9 fusion.57
  107.8 1.0 fusion.62
  108.8 0.8 fusion.55
  111.0 1.2 reshape.128
  112.2 30.1 %scatter_custom_fusion.1 = bf16[14976,128]{1,0:T(8,128)(2,1)} fusion(s32[3744]{0:T(1024)S(1)} %fusion.72, bf16[]{:T(256)} %constant.18.clone.1, bf16[3744,128]{1,0:T(8,128)(2,1)S(1)} %reshape.128, s32[4096]{0:T(1024)S(1)} %pad_clamp_fusion), kind=kCustom, calls=%fused_computation.103 | custom fusion | bytes 3833858 | tf_op jit(solution)/shard_map/scatter | solution.py:66
  142.3 5.8 reshape.134
  148.8 6.1 all-to-all-start.1
  155.1 267.2 %while.21 = (s32[]{:T(128)}, f32[8,1024,128]{2,1,0:T(8,128)}, s32[3744,19]{0,1:T(8,128)S(1)}, s32[8]{0:T(128)S(1)}, bf16[3744,128]{1,0:T(8,128)(2,1)S(1)}, /*index=5*/s32[]{:T(128)}) while((s32[]{:T(128)}, f32[8,1024,128]{2,1,0:T(8,128)}, s32[3744,19]{0,1:T(8,128)S(1)}, s32[8]{0:T(128)S(1)}, bf16[3744,128]{1,0:T(8,128)(2,1)S(1)}, ...), condition=%wide.region_2.3_spmd, body=%wide.region_1.0_spmd.sunk | while | flops 1196164096 | bytes 2344673 | solution.py:112
  155.7 0.6 iota_add_fusion.5
  156.3 0.8 slice_reduce_fusion.20
  157.1 31.4 %fusion.100 = f32[8,1024,128]{2,1,0:T(8,128)} fusion(f32[8,1024,128]{2,1,0:T(8,128)} %get-tuple-element.326, s32[]{:T(128)S(6)} %copy.44, bf16[3744,128]{1,0:T(8,128)(2,1)S(1)} %get-tuple-element.335, s32[1024]{0:T(1024)S(1)} %iota_add_fusion.5, s32[3744]{0:T(1024)S(1)} %get-tuple-element.294, s32[3744]{0:T(1024)S(1)} %get-tuple-element.295, ...), kind=kOutput, calls=%fused_computation.70.clone.2 | convolution fusion | flops 1196163072 | bytes 1771396 | tf_op jit(solution)/shard_map/while/body/eval_jaxpr/dot_general | solution.py:107
  189.1 0.6 iota_add_fusion.5
  189.7 0.8 slice_reduce_fusion.20
  190.5 31.4 %fusion.100 = f32[8,1024,128]{2,1,0:T(8,128)} fusion(f32[8,1024,128]{2,1,0:T(8,128)} %get-tuple-element.326, s32[]{:T(128)S(6)} %copy.44, bf16[3744,128]{1,0:T(8,128)(2,1)S(1)} %get-tuple-element.335, s32[1024]{0:T(1024)S(1)} %iota_add_fusion.5, s32[3744]{0:T(1024)S(1)} %get-tuple-element.294, s32[3744]{0:T(1024)S(1)} %get-tuple-element.295, ...), kind=kOutput, calls=%fused_computation.70.clone.2 | convolution fusion | flops 1196163072 | bytes 1771396 | tf_op jit(solution)/shard_map/while/body/eval_jaxpr/dot_general | solution.py:107
  222.5 0.6 iota_add_fusion.5
  223.1 0.8 slice_reduce_fusion.20
  223.9 31.4 %fusion.100 = f32[8,1024,128]{2,1,0:T(8,128)} fusion(f32[8,1024,128]{2,1,0:T(8,128)} %get-tuple-element.326, s32[]{:T(128)S(6)} %copy.44, bf16[3744,128]{1,0:T(8,128)(2,1)S(1)} %get-tuple-element.335, s32[1024]{0:T(1024)S(1)} %iota_add_fusion.5, s32[3744]{0:T(1024)S(1)} %get-tuple-element.294, s32[3744]{0:T(1024)S(1)} %get-tuple-element.295, ...), kind=kOutput, calls=%fused_computation.70.clone.2 | convolution fusion | flops 1196163072 | bytes 1771396 | tf_op jit(solution)/shard_map/while/body/eval_jaxpr/dot_general | solution.py:107
  255.9 0.6 iota_add_fusion.5
  256.5 0.8 slice_reduce_fusion.20
  257.3 31.4 %fusion.100 = f32[8,1024,128]{2,1,0:T(8,128)} fusion(f32[8,1024,128]{2,1,0:T(8,128)} %get-tuple-element.326, s32[]{:T(128)S(6)} %copy.44, bf16[3744,128]{1,0:T(8,128)(2,1)S(1)} %get-tuple-element.335, s32[1024]{0:T(1024)S(1)} %iota_add_fusion.5, s32[3744]{0:T(1024)S(1)} %get-tuple-element.294, s32[3744]{0:T(1024)S(1)} %get-tuple-element.295, ...), kind=kOutput, calls=%fused_computation.70.clone.2 | convolution fusion | flops 1196163072 | bytes 1771396 | tf_op jit(solution)/shard_map/while/body/eval_jaxpr/dot_general | solution.py:107
  289.3 0.6 iota_add_fusion.5
  289.9 0.8 slice_reduce_fusion.20
  290.7 31.4 %fusion.100 = f32[8,1024,128]{2,1,0:T(8,128)} fusion(f32[8,1024,128]{2,1,0:T(8,128)} %get-tuple-element.326, s32[]{:T(128)S(6)} %copy.44, bf16[3744,128]{1,0:T(8,128)(2,1)S(1)} %get-tuple-element.335, s32[1024]{0:T(1024)S(1)} %iota_add_fusion.5, s32[3744]{0:T(1024)S(1)} %get-tuple-element.294, s32[3744]{0:T(1024)S(1)} %get-tuple-element.295, ...), kind=kOutput, calls=%fused_computation.70.clone.2 | convolution fusion | flops 1196163072 | bytes 1771396 | tf_op jit(solution)/shard_map/while/body/eval_jaxpr/dot_general | solution.py:107
  322.7 0.6 iota_add_fusion.5
  323.3 0.8 slice_reduce_fusion.20
  324.1 31.4 %fusion.100 = f32[8,1024,128]{2,1,0:T(8,128)} fusion(f32[8,1024,128]{2,1,0:T(8,128)} %get-tuple-element.326, s32[]{:T(128)S(6)} %copy.44, bf16[3744,128]{1,0:T(8,128)(2,1)S(1)} %get-tuple-element.335, s32[1024]{0:T(1024)S(1)} %iota_add_fusion.5, s32[3744]{0:T(1024)S(1)} %get-tuple-element.294, s32[3744]{0:T(1024)S(1)} %get-tuple-element.295, ...), kind=kOutput, calls=%fused_computation.70.clone.2 | convolution fusion | flops 1196163072 | bytes 1771396 | tf_op jit(solution)/shard_map/while/body/eval_jaxpr/dot_general | solution.py:107
  356.1 0.6 iota_add_fusion.5
  356.7 0.8 slice_reduce_fusion.20
  357.5 31.4 %fusion.100 = f32[8,1024,128]{2,1,0:T(8,128)} fusion(f32[8,1024,128]{2,1,0:T(8,128)} %get-tuple-element.326, s32[]{:T(128)S(6)} %copy.44, bf16[3744,128]{1,0:T(8,128)(2,1)S(1)} %get-tuple-element.335, s32[1024]{0:T(1024)S(1)} %iota_add_fusion.5, s32[3744]{0:T(1024)S(1)} %get-tuple-element.294, s32[3744]{0:T(1024)S(1)} %get-tuple-element.295, ...), kind=kOutput, calls=%fused_computation.70.clone.2 | convolution fusion | flops 1196163072 | bytes 1771396 | tf_op jit(solution)/shard_map/while/body/eval_jaxpr/dot_general | solution.py:107
  389.5 0.6 iota_add_fusion.5
  390.1 0.8 slice_reduce_fusion.20
  390.9 31.4 %fusion.100 = f32[8,1024,128]{2,1,0:T(8,128)} fusion(f32[8,1024,128]{2,1,0:T(8,128)} %get-tuple-element.326, s32[]{:T(128)S(6)} %copy.44, bf16[3744,128]{1,0:T(8,128)(2,1)S(1)} %get-tuple-element.335, s32[1024]{0:T(1024)S(1)} %iota_add_fusion.5, s32[3744]{0:T(1024)S(1)} %get-tuple-element.294, s32[3744]{0:T(1024)S(1)} %get-tuple-element.295, ...), kind=kOutput, calls=%fused_computation.70.clone.2 | convolution fusion | flops 1196163072 | bytes 1771396 | tf_op jit(solution)/shard_map/while/body/eval_jaxpr/dot_general | solution.py:107
  422.3 2.5 convolution_bitcast_fusion
  424.8 2.6 fusion.66
  428.1 20.1 %psum.62 = f32[3456]{0:T(1024)S(1)} all-reduce(f32[3456]{0:T(1024)S(1)} %copy-done.19), channel_id=1, replica_groups=mesh['wide'=8,'narrow'=4] {'narrow'}, use_global_device_ids=true, to_apply=%region_19.20 | all-reduce | flops 3456 | bytes 27648 | tf_op jit(solution)/shard_map/psum | solution.py:121
  448.4 5.8 reshape.135
  454.2 56.6 %while.22 = (s32[]{:T(128)}, f32[4,512,128]{2,1,0:T(8,128)}, s32[32,468]{1,0:T(8,128)}, s32[4]{0:T(128)S(1)}, bf16[14976,128]{1,0:T(8,128)(2,1)}, /*index=5*/s32[14976]{0:T(1024)S(1)}, s32[]{:T(128)}) while((s32[]{:T(128)}, f32[4,512,128]{2,1,0:T(8,128)}, s32[32,468]{1,0:T(8,128)}, s32[4]{0:T(128)S(1)}, ...), condition=%wide.wide.region_12.13_spmd, body=%wide.wide.region_11.12_spmd.sunk | while | flops 1970602496 | bytes 4160105 | solution.py:97
  454.8 0.6 iota_add_fusion.6
  455.5 12.9 %fusion.103 = f32[4,512,128]{2,1,0:T(8,128)} fusion(f32[4,512,128]{2,1,0:T(8,128)} %get-tuple-element.345, s32[]{:T(128)S(6)} %copy.54, bf16[14976,128]{1,0:T(8,128)(2,1)} %get-tuple-element.355, s32[512]{0:T(512)S(1)} %iota_add_fusion.6, s32[14976]{0:T(1024)S(1)} %get-tuple-element.356), kind=kOutput, calls=%fused_computation.10.clone.clone.1 | convolution fusion | flops 1970601984 | bytes 4157956 | tf_op jit(solution)/shard_map/while/body/eval_jaxpr/dot_general | solution.py:92
  469.0 0.6 iota_add_fusion.6
  469.6 12.9 %fusion.103 = f32[4,512,128]{2,1,0:T(8,128)} fusion(f32[4,512,128]{2,1,0:T(8,128)} %get-tuple-element.345, s32[]{:T(128)S(6)} %copy.54, bf16[14976,128]{1,0:T(8,128)(2,1)} %get-tuple-element.355, s32[512]{0:T(512)S(1)} %iota_add_fusion.6, s32[14976]{0:T(1024)S(1)} %get-tuple-element.356), kind=kOutput, calls=%fused_computation.10.clone.clone.1 | convolution fusion | flops 1970601984 | bytes 4157956 | tf_op jit(solution)/shard_map/while/body/eval_jaxpr/dot_general | solution.py:92
  483.1 0.6 iota_add_fusion.6
  483.8 12.9 %fusion.103 = f32[4,512,128]{2,1,0:T(8,128)} fusion(f32[4,512,128]{2,1,0:T(8,128)} %get-tuple-element.345, s32[]{:T(128)S(6)} %copy.54, bf16[14976,128]{1,0:T(8,128)(2,1)} %get-tuple-element.355, s32[512]{0:T(512)S(1)} %iota_add_fusion.6, s32[14976]{0:T(1024)S(1)} %get-tuple-element.356), kind=kOutput, calls=%fused_computation.10.clone.clone.1 | convolution fusion | flops 1970601984 | bytes 4157956 | tf_op jit(solution)/shard_map/while/body/eval_jaxpr/dot_general | solution.py:92
  498.0 12.9 %fusion.103 = f32[4,512,128]{2,1,0:T(8,128)} fusion(f32[4,512,128]{2,1,0:T(8,128)} %get-tuple-element.345, s32[]{:T(128)S(6)} %copy.54, bf16[14976,128]{1,0:T(8,128)(2,1)} %get-tuple-element.355, s32[512]{0:T(512)S(1)} %iota_add_fusion.6, s32[14976]{0:T(1024)S(1)} %get-tuple-element.356), kind=kOutput, calls=%fused_computation.10.clone.clone.1 | convolution fusion | flops 1970601984 | bytes 4157956 | tf_op jit(solution)/shard_map/while/body/eval_jaxpr/dot_general | solution.py:92
  510.9 1.7 multiply_reduce_fusion.1
  512.6 301.7 %all-reduce.8.cloned.1.call-done = (f32[8192,128]{1,0:T(8,128)}, f32[3456,256]{1,0:T(8,128)}, f32[3456,256]{0,1:T(8,128)}) async-done(((f32[8192,128]{1,0:T(8,128)}, f32[3456,256]{1,0:T(8,128)}, f32[3456,256]{0,1:T(8,128)}), (f32[8192,128]{1,0:T(8,128)}, f32[3456,256]{1,0:T(8,128)}, f32[3456,256]{0,1:T(8,128)})) %all-reduce.8.cloned.1.call-update) | async-done | bytes 11272208 | tf_op jit(solution)/shard_map/psum | solution.py:121
  814.3 1.3 fusion.64
  815.7 188.3 %all-reduce.9 = (bf16[3456,256]{1,0:T(8,128)(2,1)}, bf16[3456,256]{0,1:T(8,128)(2,1)S(1)}, f32[3456]{0:T(1024)}) all-reduce(f32[3456,256]{1,0:T(8,128)} %get-tuple-element.151, f32[3456,256]{0,1:T(8,128)} %get-tuple-element.152, f32[3456]{0:T(1024)S(1)} %psum.62), channel_id=1, replica_groups=mesh['wide'=8,'narrow'=4] {'wide'}, use_global_device_ids=true, to_apply=%region_15.16 | all-reduce | flops 1772928 | bytes 10644480 | tf_op jit(solution)/shard_map/psum | solution.py:120
  1003.9 2.2 copy.35
  1006.2 3.5 multiply_reduce_fusion
  1009.7 4.3 divide_subtract_fusion
  (100 shorter events, 12.4 us)
Async XLA Ops:
  7.2 99.1 %copy-start = (bf16[3456,256]{1,0:T(8,128)(2,1)S(1)}, bf16[3456,256]{1,0:T(8,128)(2,1)}, u32[]{:S(2)}) copy-start(bf16[3456,256]{1,0:T(8,128)(2,1)} %param.19) | copy-start | bytes 5308420
  16.0 41.3 %copy-start.21 = (s32[144,26]{0,1:T(8,128)S(1)}, s32[144,26]{0,1:T(8,128)}, u32[]{:S(2)}) copy-start(s32[144,26]{0,1:T(8,128)} %param.29) | copy-start | bytes 44932
  57.6 46.7 %copy-start.2 = (bf16[144,3456]{1,0:T(8,128)(2,1)S(1)}, bf16[144,3456]{1,0:T(8,128)(2,1)}, u32[]{:S(2)}) copy-start(bf16[144,3456]{1,0:T(8,128)(2,1)} %param.17) | copy-start | bytes 2985988
  57.6 48.7 %copy-start.17 = (f32[3456]{0:T(1024)S(1)}, f32[3456]{0:T(1024)}, u32[]{:S(2)}) copy-start(f32[3456]{0:T(1024)} %param.22) | copy-start | bytes 41476
  57.6 48.7 %copy-start.22 = (f32[3456]{0:T(1024)S(1)}, f32[3456]{0:T(1024)}, u32[]{:S(2)}) copy-start(f32[3456]{0:T(1024)} %param.21) | copy-start | bytes 41476
  96.5 51.7 %all-to-all-start = ((s32[32,1,468]{2,1,0:T(1,128)}), s32[32,1,468]{2,1,0:T(1,128)S(1)}, u32[]{:S(2)}, u32[]{:S(2)}) async-start(s32[32,1,468]{2,1,0:T(1,128)} %all_to_all.11), calls=%async_computation | async-start | bytes 131072 | tf_op jit(solution)/shard_map/all_to_all | solution.py:77
  104.3 2.9 copy-start.26
  106.3 1.5 copy-start.9
  107.2 1.6 copy-start.5
  107.2 0.6 copy-start.23
  107.8 1.0 copy-start.12
  108.8 1.1 copy-start.11
  112.2 35.9 %copy-start.7 = (bf16[3744,128]{1,0:T(8,128)(2,1)}, bf16[3744,128]{1,0:T(8,128)(2,1)S(1)}, u32[]{:S(2)}) copy-start(bf16[3744,128]{1,0:T(8,128)(2,1)S(1)} %reshape.128) | copy-start | bytes 2875396
  148.1 6.9 copy-start.8
  148.1 0.6 copy-start.14
  148.8 299.6 %all-to-all-start.1 = ((bf16[32,468,128]{2,1,0:T(8,128)(2,1)}), bf16[32,468,128]{2,1,0:T(8,128)(2,1)}, u32[]{:S(2)}, u32[]{:S(2)}) async-start(bf16[32,468,128]{2,1,0:T(8,128)(2,1)} %reshape.134), calls=%async_computation.1 | async-start | bytes 7733248 | tf_op jit(solution)/shard_map/all_to_all | solution.py:70
  154.8 659.5 %all-reduce.8.cloned.1.call-start = ((), (), s32[]{:S(2)}) async-start(), calls=%async_computation.3 | async-start | bytes 22544384 | tf_op jit(solution)/shard_map/psum | solution.py:121
  155.1 267.2 %copy-start.3 = (bf16[144,3456]{1,0:T(8,128)(2,1)S(1)}, bf16[144,3456]{1,0:T(8,128)(2,1)}, u32[]{:S(2)}) copy-start(bf16[144,3456]{1,0:T(8,128)(2,1)} %param.17) | copy-start | bytes 2985988
  155.1 267.2 %copy-start.13 = (bf16[144,256]{1,0:T(8,128)(2,1)S(1)}, bf16[144,256]{1,0:T(8,128)(2,1)}, u32[]{:S(2)}) copy-start(bf16[144,256]{1,0:T(8,128)(2,1)} %copy-done.12) | copy-start | bytes 221188
  422.3 2.5 copy-start.10
  422.3 2.5 copy-start.18
  422.3 2.5 copy-start.24
  427.4 0.7 copy-start.19
  427.4 20.8 %copy-start.15 = (s32[32,1,468]{2,1,0:T(1,128)S(1)}, s32[32,1,468]{2,1,0:T(1,128)}, u32[]{:S(2)}) copy-start(s32[32,1,468]{2,1,0:T(1,128)} %copy-done.14) | copy-start | bytes 179716
  427.4 578.7 %all-reduce.6.cloned.1.call-start = ((), (), s32[]{:S(2)}) async-start(), calls=%async_computation.2 | async-start | bytes 8388608 | tf_op jit(solution)/shard_map/psum | solution.py:120
  448.2 6.0 copy-start.16
  454.2 58.3 %copy-start.25 = (f32[2048]{0:T(1024)S(1)}, f32[2048]{0:T(1024)}, u32[]{:S(2)}) copy-start(f32[2048]{0:T(1024)} %param.26) | copy-start | bytes 24580
  510.9 303.5 %copy-start.6 = (f32[2048,128]{1,0:T(8,128)S(1)}, f32[2048,128]{1,0:T(8,128)}, u32[]{:S(2)}) copy-start(f32[2048,128]{1,0:T(8,128)} %param.25) | copy-start | bytes 3145732
  1003.9 5.7 copy-start.20
  1006.1 3.5 copy-start.4
  1009.7 4.4 copy-start.1
Sparse Core Ops, SparseCore 0:
  427.5 386.7 all-reduce.7
  817.6 122.0 all-reduce.5
